TPU v7x, 256 devices: a whole 4x4x8 slice. The times are simulated.
256 devices in a mesh: dp: 32 (over y, z), tensor: 8 (over x, core).
Axes of the slice: x: 4, y: 4, z: 8, core: 2. Of those that a mesh axis runs over, the one named last changes fastest.
Arguments:
- queries: bfloat16 [8192, 8192], P('dp', 'tensor')
- keys: bfloat16 [8192, 1024], P('dp', 'tensor')
- values: bfloat16 [8192, 1024], P('dp', 'tensor'), may hold values from -6 to 6
- prompt_keys: bfloat16 [4096, 1024], P('dp', 'tensor'), may hold values from -6 to 6
- prompt_values: bfloat16 [4096, 1024], P('dp', 'tensor'), may hold values from -6 to 6
- lengths: int32 [32, 4], P('dp'), may hold values from 1 to 128, 256 in all within a row
- owner_slice: int32 [32], replicated, may hold values from 0 to 31, each once
- device_group: int32 [32], replicated, may hold values from 0 to 7
- out_weight: bfloat16 [8192, 5120], P('tensor'), may hold values from -0.0625 to 0.0625
- cotangent: bfloat16 [8192, 5120], P('dp', 'tensor'), may hold values from -6 to 6
Outputs:
- block_out: bfloat16 [8192, 5120], P(('dp', 'tensor'))
- grad_queries: bfloat16 [8192, 8192], P('dp', 'tensor')
- grad_keys: bfloat16 [8192, 1024], P('dp', 'tensor')
- grad_values: bfloat16 [8192, 1024], P('dp', 'tensor')
- grad_prompt_keys: float32 [4096, 1024], P('dp', 'tensor')
- grad_prompt_values: float32 [4096, 1024], P('dp', 'tensor')
Inputs may be any that keep to these rules, and one draw needn't show every extreme that they name: Each row holds 4 lengths that sum to 256; its largest is exactly half of 256. `owner_slice`: a permutation of the 32 prompt slices.
All inputs are finite; a program needn't handle non-finite values.
Results may differ from a plain program's by a relative error of at most 0.034.
Values may be sent and summed in bfloat16 or wider, within the bound.
A program may use at most 128 MiB of HBM per device.

v0:
```python
import jax
import jax.numpy as jnp
from jax import lax
from jax.sharding import PartitionSpec as P

HEAD = 128
PIECES = 4


def local(
    queries,
    keys,
    values,
    prompt_keys,
    prompt_values,
    lengths,
    owner_slice,
    device_group,
    out_weight,
    cotangent,
):
    rows = queries.shape[0]
    kv_width = keys.shape[1]
    kv_local = kv_width // HEAD
    q_local = queries.shape[1] // HEAD
    ratio = q_local // kv_local
    slice_rows = prompt_keys.shape[0]
    prompt_rows = slice_rows * PIECES
    scale = HEAD ** (-0.5)
    group = device_group[lax.axis_index("dp")]
    pieces = (
        lax.all_gather(prompt_keys, "dp", axis=0, tiled=True),
        lax.all_gather(prompt_values, "dp", axis=0, tiled=True),
    )
    count = pieces[0].shape[0]
    spot = jnp.arange(count, dtype=jnp.int32)
    held = owner_slice[spot // slice_rows]
    target = held % PIECES * slice_rows + spot % slice_rows
    match = held // PIECES == group
    select = (
        (target[None, :] == jnp.arange(prompt_rows, dtype=jnp.int32)[:, None]) & match[None, :]
    ).astype(jnp.bfloat16)
    got_keys = jnp.dot(select, pieces[0], preferred_element_type=jnp.float32)
    got_values = jnp.dot(select, pieces[1], preferred_element_type=jnp.float32)
    all_keys = jnp.concatenate([got_keys.astype(jnp.bfloat16), keys], 0).reshape(
        prompt_rows + rows, kv_local, HEAD
    )
    all_values = jnp.concatenate([got_values.astype(jnp.bfloat16), values], 0).reshape(
        prompt_rows + rows, kv_local, HEAD
    )
    ends = jnp.cumsum(lengths[0])
    position = jnp.arange(rows, dtype=jnp.int32)
    segment = jnp.sum((position[:, None] >= ends[None, :]).astype(jnp.int32), 1)
    inside = (segment[:, None] == segment[None, :]) & (position[None, :] <= position[:, None])
    mask = jnp.concatenate([jnp.ones((rows, prompt_rows), bool), inside], 1)
    q_heads = queries.reshape(rows, kv_local, ratio, HEAD)
    scores = (
        jnp.einsum("rkgd,nkd->kgrn", q_heads, all_keys, preferred_element_type=jnp.float32) * scale
    )
    scores = jnp.where(mask[None, None], scores, jnp.float32(-1e30))
    top = jnp.max(scores, -1, keepdims=True)
    expo = jnp.exp(scores - top)
    probs = expo / jnp.sum(expo, -1, keepdims=True)
    probs_low = probs.astype(jnp.bfloat16)
    attended = jnp.einsum(
        "kgrn,nkd->rkgd", probs_low, all_values, preferred_element_type=jnp.float32
    )
    attended = attended.astype(jnp.bfloat16).reshape(rows, q_local * HEAD)
    block_out = lax.psum_scatter(
        jnp.dot(attended, out_weight, preferred_element_type=jnp.float32),
        "tensor",
        scatter_dimension=0,
        tiled=True,
    ).astype(jnp.bfloat16)
    grad_att = lax.dot_general(
        lax.all_gather(cotangent, "tensor", axis=1, tiled=True),
        out_weight,
        (((1,), (1,)), ((), ())),
        preferred_element_type=jnp.float32,
    )
    grad_att = grad_att.astype(jnp.bfloat16)
    grad_heads = grad_att.reshape(rows, kv_local, ratio, HEAD)
    delta = jnp.sum(
        grad_heads.astype(jnp.float32)
        * attended.reshape(rows, kv_local, ratio, HEAD).astype(jnp.float32),
        -1,
    )
    delta = jnp.transpose(delta, (1, 2, 0))
    grad_probs = jnp.einsum(
        "rkgd,nkd->kgrn", grad_heads, all_values, preferred_element_type=jnp.float32
    )
    grad_scores = (probs * (grad_probs - delta[..., None])).astype(jnp.bfloat16)
    grad_q = (
        jnp.einsum("kgrn,nkd->rkgd", grad_scores, all_keys, preferred_element_type=jnp.float32)
        * scale
    )
    grad_q = grad_q.astype(jnp.bfloat16).reshape(rows, q_local * HEAD)
    grad_k = (
        jnp.einsum("kgrn,rkgd->nkd", grad_scores, q_heads, preferred_element_type=jnp.float32)
        * scale
    )
    grad_k = grad_k.reshape(prompt_rows + rows, kv_width)
    grad_v = jnp.einsum("kgrn,rkgd->nkd", probs_low, grad_heads, preferred_element_type=jnp.float32)
    grad_v = grad_v.reshape(prompt_rows + rows, kv_width)
    partial_value = jnp.concatenate([grad_k[:prompt_rows], grad_v[:prompt_rows]], 1)
    spot = jnp.arange(slice_rows * lax.axis_size("dp"), dtype=jnp.int32)
    held = owner_slice[spot // slice_rows]
    source = held % PIECES * slice_rows + spot % slice_rows
    match = held // PIECES == group
    summed = lax.psum_scatter(
        jnp.where(match[:, None], jnp.take(partial_value, source, axis=0), jnp.float32(0.0)).astype(
            jnp.bfloat16
        ),
        "dp",
        scatter_dimension=0,
        tiled=True,
    ).astype(jnp.float32)
    return (
        block_out,
        grad_q,
        grad_k[prompt_rows:].astype(jnp.bfloat16),
        grad_v[prompt_rows:].astype(jnp.bfloat16),
        summed[:, :kv_width],
        summed[:, kv_width:],
    )


def solution(mesh):
    placed = (
        P("dp", "tensor"),
        P("dp", "tensor"),
        P("dp", "tensor"),
        P("dp", "tensor"),
        P("dp", "tensor"),
        P("dp", None),
        P(),
        P(),
        P("tensor", None),
        P("dp", "tensor"),
    )
    return jax.shard_map(
        local,
        mesh=mesh,
        in_specs=placed,
        out_specs=(
            P(("dp", "tensor"), None),
            P("dp", "tensor"),
            P("dp", "tensor"),
            P("dp", "tensor"),
            P("dp", "tensor"),
            P("dp", "tensor"),
        ),
        check_vma=False,
    )
```

profile of v0, /device:TPU:1, one launch (start us, length us, event | category | flops | bytes accessed | tf_op | source)
XLA Modules:
  0.0 503.0 jit_solution(5597691473889496112)
XLA Ops:
  9.4 1.8 fusion.48
  11.2 2.1 fusion.47
  18.4 4.3 compare_select_fusion.4
  22.8 16.5 %compare_and_fusion = (pred[4096]{0:T(1024)(128)(4,1)}, s32[4096]{0:T(1024)S(1)}, s32[4096]{0:T(1024)S(1)}) fusion(pred[4096]{0:T(1024)(128)(4,1)S(1)} %compare_reduce_fusion, pred[4096]{0:T(1024)(128)(4,1)S(1)} %compare_reduce_fusion.1, pred[4096]{0:T(1024)(128)(4,1)S(1)} %compare_reduce_fusion.2, pred[4096]{0:T(1024)(128)(4,1)S(1)} %compare_reduce_fusion.3, ...), kind=kLoop, calls=%fused_computation.106 | loop fusion | flops 204800 | bytes 155748 | tf_op jit(solution)/shard_map/jit(_take)/and | solution.py:111
  40.6 45.6 %all-gather.6.cloned.1.call-done = bf16[4096,128]{1,0:T(8,128)(2,1)} async-done(((bf16[128,128]{1,0:T(8,128)(2,1)}), bf16[4096,128]{1,0:T(8,128)(2,1)}) %all-gather.6.cloned.1.call-update) | async-done | bytes 1048592 | tf_op jit(solution)/shard_map/all_gather | solution.py:32
  86.2 2.9 fusion.21
  92.9 1.5 convert_bitcast_fusion
  94.3 3.8 copy.55
  98.1 64.5 %all-gather.4.cloned.1.call-done = bf16[4096,128]{1,0:T(8,128)(2,1)} async-done(((bf16[128,128]{1,0:T(8,128)(2,1)}), bf16[4096,128]{1,0:T(8,128)(2,1)}) %all-gather.4.cloned.1.call-update) | async-done | bytes 1048592 | tf_op jit(solution)/shard_map/all_gather | solution.py:33
  162.7 3.6 fusion.18
  166.2 29.7 %all-gather.8.cloned.1.call-done = bf16[256,5120]{1,0:T(8,128)(2,1)} async-done(((bf16[256,640]{1,0:T(8,128)(2,1)}), bf16[256,5120]{1,0:T(8,128)(2,1)}) %all-gather.8.cloned.1.call-update) | async-done | bytes 2621456 | tf_op jit(solution)/shard_map/all_gather | solution.py:76
  195.9 8.5 %convolution_convert_fusion = bf16[256,1024]{1,0:T(8,128)(2,1)} fusion(bf16[256,5120]{1,0:T(8,128)(2,1)} %all-gather.8.cloned.1.call-done, bf16[1024,5120]{1,0:T(8,128)(2,1)} %param.18), kind=kOutput, calls=%fused_computation.21 | convolution fusion | flops 2684616704 | bytes 13631488 | tf_op jit(solution)/shard_map/dot_general | solution.py:75
  204.4 2.2 copy.50
  206.6 2.8 multiply_reduce_fusion
  209.4 5.3 %fusion.14 = bf16[8,256,768]{1,2,0:T(8,128)(2,1)S(1)} fusion(f32[8,256]{1,0:T(8,128)S(1)} %bitcast.155, f32[8,256]{1,0:T(8,128)S(1)} %fusion.8, f32[8,256]{1,0:T(8,128)S(1)} %get-tuple-element.61, f32[768,256,8]{1,0,2:T(8,128)} %copy-done, pred[256,768]{0,1:T(8,128)(4,1)S(1)} %concatenate.13, bf16[256,128]{1,0:T(8,128)(2,1)} %param.12, ...), kind=kOutput, calls=%fused_computation.18 | convolution fusion | flops 414056448 | bytes 10379264 | tf_op jit(solution)/shard_map/rkgd,nkd->kgrn/dot_general | solution.py:89
  216.0 1.8 copy-done.1
  218.7 14.6 %gather_fusion = bf16[4096,256]{1,0:T(8,128)(2,1)S(1)} fusion(bf16[512,256]{1,0:T(8,128)(2,1)S(1)} %copy.56, s32[4096]{0:T(1024)S(1)} %copy-done.9), kind=kCustom, calls=%fused_computation | custom fusion | bytes 4210688 | tf_op jit(solution)/shard_map/jit(_take)/gather | solution.py:111
  233.3 4.2 select_convert_fusion
  237.8 9.5 %fusion.49 = f32[256,5120]{1,0:T(8,128)} fusion(bf16[256,1024]{0,1:T(8,128)(2,1)} %bitcast.146, bf16[1024,5120]{1,0:T(8,128)(2,1)} %param.18), kind=kOutput, calls=%fused_computation.118 | convolution fusion | flops 2684354560 | bytes 16252928 | tf_op jit(solution)/shard_map/dot_general | solution.py:70
  247.4 1.4 fusion.15
  248.8 2.1 copy.57
  253.2 195.6 %reduce-scatter.5.cloned.1.call-done = bf16[128,256]{1,0:T(8,128)(2,1)} async-done(((bf16[4096,256]{1,0:T(8,128)(2,1)}), bf16[128,256]{1,0:T(8,128)(2,1)}) %reduce-scatter.5.cloned.1.call-update) | async-done | bytes 65552 | tf_op jit(solution)/shard_map/reduce_scatter | solution.py:110
  450.2 44.4 %reduce-scatter.3.cloned.1.call-done = f32[32,5120]{1,0:T(8,128)} async-done(((f32[256,5120]{1,0:T(8,128)}), f32[32,5120]{1,0:T(8,128)}) %reduce-scatter.3.cloned.1.call-update) | async-done | bytes 655376 | tf_op jit(solution)/shard_map/reduce_scatter | solution.py:69
  494.6 1.8 convert_element_type.78
  (84 shorter events, 18.5 us)
Async XLA Ops:
  7.2 81.9 %copy-start.7 = (bf16[256,128]{1,0:T(8,128)(2,1)S(1)}, bf16[256,128]{1,0:T(8,128)(2,1)}, u32[]{:S(2)}) copy-start(bf16[256,128]{1,0:T(8,128)(2,1)} %param.11) | copy-start | bytes 196612
  7.2 79.1 %all-gather.6.cloned.1.call-start = ((), (), s32[]{:S(2)}) async-start(), calls=%async_computation.3 | async-start | bytes 1081344 | tf_op jit(solution)/shard_map/all_gather | solution.py:32
  7.9 154.7 %all-gather.4.cloned.1.call-start = ((), (), s32[]{:S(2)}) async-start(), calls=%async_computation.2 | async-start | bytes 1081344 | tf_op jit(solution)/shard_map/all_gather | solution.py:33
  8.7 187.2 %all-gather.8.cloned.1.call-start = ((), (), s32[]{:S(2)}) async-start(), calls=%async_computation.5 | async-start | bytes 2949120 | tf_op jit(solution)/shard_map/all_gather | solution.py:76
  9.4 439.4 %reduce-scatter.5.cloned.1.call-start = ((), (), s32[]{:S(2)}) async-start(), calls=%async_computation.6 | async-start | bytes 2162688 | tf_op jit(solution)/shard_map/reduce_scatter | solution.py:110
  17.0 73.2 %copy-start.5 = (bf16[256,1024]{0,1:T(8,128)(2,1)}, bf16[256,1024]{0,1:T(8,128)(2,1)S(1)}, u32[]{:S(2)}) copy-start(bf16[256,1024]{0,1:T(8,128)(2,1)S(1)} %copy.67) | copy-start | bytes 1572868
  39.3 50.9 %copy-start.10 = (s32[4096]{0:T(1024)}, s32[4096]{0:T(1024)S(1)}, u32[]{:S(2)}) copy-start(s32[4096]{0:T(1024)S(1)} %get-tuple-element.25) | copy-start | bytes 49156
  39.9 50.3 %copy-start.11 = (pred[4096]{0:T(1024)(128)(4,1)}, pred[4096]{0:T(1024)(128)(4,1)S(1)}, u32[]{:S(2)}) copy-start(pred[4096]{0:T(1024)(128)(4,1)S(1)} %fusion.33) | copy-start | bytes 12292
  90.2 2.7 copy-start
  209.4 5.3 %copy-start.6 = (bf16[256,1024]{0,1:T(8,128)(2,1)S(1)}, bf16[256,1024]{0,1:T(8,128)(2,1)}, u32[]{:S(2)}) copy-start(bf16[256,1024]{0,1:T(8,128)(2,1)} %copy-done.5) | copy-start | bytes 1572868
  209.4 6.5 %copy-start.4 = (bf16[256,1024]{1,0:T(8,128)(2,1)S(1)}, bf16[256,1024]{1,0:T(8,128)(2,1)}, u32[]{:S(2)}) copy-start(bf16[256,1024]{1,0:T(8,128)(2,1)} %convolution_convert_fusion) | copy-start | bytes 1572868
  214.7 3.8 copy-start.2
  214.7 3.1 copy-start.1
  214.7 4.0 copy-start.9
  215.8 2.7 copy-start.8
  218.6 14.6 %copy-start.12 = (pred[4096]{0:T(1024)(128)(4,1)S(1)}, pred[4096]{0:T(1024)(128)(4,1)}, u32[]{:S(2)}) copy-start(pred[4096]{0:T(1024)(128)(4,1)} %copy-done.11) | copy-start | bytes 12292
  218.7 14.6 %copy-start.13 = (pred[4096]{0:T(1024)(128)(4,1)S(1)}, pred[4096]{0:T(1024)(128)(4,1)}, u32[]{:S(2)}) copy-start(pred[4096]{0:T(1024)(128)(4,1)} %get-tuple-element.24) | copy-start | bytes 12292
  237.5 257.1 %reduce-scatter.3.cloned.1.call-start = ((), (), s32[]{:S(2)}) async-start(), calls=%async_computation.4 | async-start | bytes 5898240 | tf_op jit(solution)/shard_map/reduce_scatter | solution.py:69
  237.8 9.6 %copy-start.3 = (bf16[8,256,768]{1,2,0:T(8,128)(2,1)S(1)}, bf16[8,256,768]{1,2,0:T(8,128)(2,1)}, u32[]{:S(2)}) copy-start(bf16[8,256,768]{1,2,0:T(8,128)(2,1)} %copy-done.2) | copy-start | bytes 9437188
Sparse Core Ops, SparseCore 0:
  10.6 75.5 all-gather.5
  88.8 73.7 all-gather.3
  164.5 31.3 all-gather.7
  237.6 211.1 reduce-scatter.4
  451.4 43.2 reduce-scatter.2
where the time goes:
time: 506 us; the launch traced here: 503 us
  waiting for transfers between devices  382 us (75%)
  matrix products  36.8 us (7%)
  local copies, waits for them, and re-layouts  36.4 us (7%)
  other arithmetic  33.4 us (7%)
  between operations  14.1 us (3%)
    reduce_scatter x1, waiting for transfers between devices, local(): lax.psum_scatter(jnp.where(match[:, None], jnp.take(partial_value, source...  196 us
    all_gather x1, waiting for transfers between devices, local(): lax.all_gather(prompt_values, 'dp', axis=0, tiled=True)  64.5 us
    all_gather x1, waiting for transfers between devices, local(): lax.all_gather(prompt_keys, 'dp', axis=0, tiled=True)  45.6 us
    reduce_scatter x1, waiting for transfers between devices, local(): lax.psum_scatter(jnp.dot(attended, out_weight, preferred_element_type=jnp...  44.4 us
    all_gather x1, waiting for transfers between devices, local(): lax.all_gather(cotangent, 'tensor', axis=1, tiled=True)  29.7 us
    and x1, other arithmetic, local(): jnp.take(partial_value, source, axis=0)  16.5 us
    gather x1, local copies, waits for them, and re-layouts, local(): jnp.take(partial_value, source, axis=0)  14.6 us
  transfers between devices with their start and end apart: 5, of which 5 were waited for; matrix products, arithmetic and copies ran while one was open for 12% of the time, Pallas kernels for 0%

commit v1 on v0

v1 whole, which is shorter than its diff:
```python
import functools

import jax
import jax.numpy as jnp
from jax import lax
from jax.experimental import pallas as pl
from jax.experimental.pallas import tpu as pltpu
from jax.sharding import PartitionSpec as P

Y, Z, X = 4, 8, 4
HEAD = 128
HEADS = 8
ROWS = 256
PROMPT = 512
KEYS = PROMPT + ROWS
D = 5120
BLK = D // 8
PAIR = 2 * BLK
CH = 4
CW = D // CH
SUB = 256
SCALE = HEAD**-0.5
EXP_SCALE = SCALE * 1.4426950408889634
MASKED = -1e30 / SCALE
MESH = pl.DeviceIdType.MESH
F32, BF16 = jnp.float32, jnp.bfloat16
NT = (((1,), (1,)), ((), ()))
NN = (((1,), (0,)), ((), ()))


def dot(a, b, dims=NN):
    return lax.dot_general(a, b, dims, preferred_element_type=F32)


def kernel(
    len_s, own_s, grp_s,
    q_h, k_h, v_h, pk_h, pv_h, w_h, cot_h,
    bo_h, gq_h, gk_h, gv_h, gpk_h, gpv_h,
    w_s, cot_s, ga_acc, ga_t, q3, kall, vall, kt_s, vt_s, parts_k, parts_v, pick_k, pick_v,
    mask_s, pt_s, ds_s, delta_s, att_s, dk_acc, dv_acc, gq_s, gkv_s,
    g_k, g_v, rg_k, rg_v, qs_k, qs_v, rq_k, rq_v, u_k, u_v, fin_k, fin_v, out_k, out_v,
    pb, rb1, acc, rs1, rs2, bo_s, inv_s,
    loc, z1s, z1r, y2s, y2r, z3s, z3r, xs, xr, ps, pr,
    b3s, b3r, b2s, b2r, b1s, b1r, cs, cr, r1s, r1r, r2s, r2r,
):
    me = lax.axis_index("dp")
    t = lax.axis_index("tensor")
    y, z = me // Z, me % Z
    x, c = t // 2, t % 2
    right = lax.rem(x + 1, X)
    left = lax.rem(x + X - 1, X)
    opp = lax.rem(x + 2, X)

    def at_z(d):
        return (y * Z + lax.rem(z + d, Z), t)

    def at_y(d):
        return (lax.rem(y + d, Y) * Z + z, t)

    to_right = (me, right * 2 + c)
    to_left = (me, left * 2 + c)
    partner = (me, x * 2 + 1 - c)
    sent = []

    def send(src, dst, ss, rs, dev):
        cp = pltpu.make_async_remote_copy(
            src_ref=src, dst_ref=dst, send_sem=ss, recv_sem=rs, device_id=dev, device_id_type=MESH
        )
        cp.start()
        sent.append(cp)
        return cp

    lane = pl.ds(pl.multiple_of(c * BLK, 128), BLK)
    loads = [
        pltpu.make_async_copy(cot_h, cot_s.at[x, :, lane], loc.at[0]),
        pltpu.make_async_copy(k_h, kall.at[pl.ds(4, 2)], loc.at[1]),
        pltpu.make_async_copy(v_h, vall.at[pl.ds(4, 2)], loc.at[2]),
        pltpu.make_async_copy(pk_h.at[z], parts_k.at[me], loc.at[3]),
        pltpu.make_async_copy(pv_h.at[z], parts_v.at[me], loc.at[4]),
        pltpu.make_async_copy(w_h, w_s, loc.at[5]),
    ]
    for h in range(HEADS):
        loads.append(
            pltpu.make_async_copy(q_h.at[:, pl.ds(h * HEAD, HEAD)], q3.at[h], loc.at[6 + h])
        )
    for cp in loads:
        cp.start()

    barrier = pltpu.get_barrier_semaphore()
    peers = [at_z(d) for d in range(1, Z)] + [at_y(d) for d in range(1, Y)]
    peers += [to_right, to_left, partner]
    for dev in peers:
        pl.semaphore_signal(barrier, inc=1, device_id=dev, device_id_type=MESH)
    pl.semaphore_wait(barrier, len(peers))

    z1 = []
    for kv, (src, dst) in enumerate(((pk_h, parts_k), (pv_h, parts_v))):
        z1.append(
            [
                send(src.at[lax.rem(z + d, Z)], dst.at[me], z1s.at[kv, d], z1r.at[kv, d], at_z(d))
                for d in range(1, Z)
            ]
        )
    lo, hi = pl.ds(0, 128), pl.ds(128, 128)
    own_cot = cot_s.at[x]
    ra = send(cot_h.at[lo], own_cot.at[lo, lane], xs.at[0], xr.at[0], to_right)
    lb = send(cot_h.at[hi], own_cot.at[hi, lane], xs.at[1], xr.at[1], to_left)
    rb = send(cot_h.at[hi], own_cot.at[hi, lane], xs.at[2], xr.at[2], to_right)
    la = send(cot_h.at[lo], own_cot.at[lo, lane], xs.at[3], xr.at[3], to_left)
    p_own = send(cot_h, own_cot.at[:, lane], ps.at[0], pr.at[0], partner)

    def find(s, _):
        def scan(j, found):
            return jnp.where(own_s[j] == s, j, found)

        inv_s[s] = lax.fori_loop(0, Y * Z, scan, jnp.int32(0), unroll=True)
        return 0

    lax.fori_loop(0, Y * Z, find, 0)

    key_at = lax.broadcasted_iota(jnp.int32, (ROWS, ROWS), 0)
    query_at = lax.broadcasted_iota(jnp.int32, (ROWS, ROWS), 1)
    end0 = len_s[0, 0]
    end1 = end0 + len_s[0, 1]
    end2 = end1 + len_s[0, 2]

    def segment(at):
        return (
            (at >= end0).astype(jnp.int32)
            + (at >= end1).astype(jnp.int32)
            + (at >= end2).astype(jnp.int32)
        )

    seen = (segment(key_at) == segment(query_at)) & (key_at <= query_at)
    mask_s[...] = seen.astype(jnp.int32)
    dk_acc[...] = jnp.zeros_like(dk_acc)
    dv_acc[...] = jnp.zeros_like(dv_acc)

    def forward(block, rows, i, s):
        ref = cot_s.at[block, rows, lane]
        return send(ref, ref, ps.at[s], pr.at[s], partner)

    ra.wait_recv()
    ref = cot_s.at[left, lo, lane]
    fr = send(ref, ref, xs.at[4], xr.at[4], to_right)
    p_la = forward(left, lo, 0, 1)
    lb.wait_recv()
    ref = cot_s.at[right, hi, lane]
    fl = send(ref, ref, xs.at[5], xr.at[5], to_left)
    p_rb = forward(right, hi, 0, 2)

    y2 = []
    for kv, ref in enumerate((parts_k, parts_v)):
        loads[3 + kv].wait()
        for cp in z1[kv]:
            cp.wait_recv()
        rows = ref.at[pl.ds(y * Z, Z)]
        y2.append([send(rows, rows, y2s.at[kv, d], y2r.at[kv, d], at_y(d)) for d in range(1, Y)])

    def grad_att(block, first):
        cols = pl.ds(pl.multiple_of(block * PAIR, 128), PAIR)

        def step(i, _):
            rows = pl.ds(pl.multiple_of(i * 512, 512), 512)
            part = dot(w_s[rows, cols], cot_s[block], NT)
            ga_acc[rows, :] = part if first else ga_acc[rows, :] + part
            return 0

        lax.fori_loop(0, 2, step, 0)

    loads[0].wait()
    loads[5].wait()
    p_own.wait_recv()
    grad_att(x, True)

    rb.wait_recv()
    p_lb = forward(left, hi, 0, 3)
    la.wait_recv()
    p_ra = forward(right, lo, 0, 4)

    z3 = []
    for kv, (ref, pick, full) in enumerate(((parts_k, pick_k, kall), (parts_v, pick_v, vall))):
        for cp in y2[kv]:
            cp.wait_recv()

        def choose(dest, _, ref=ref, pick=pick):
            first = grp_s[y * Z + dest] * 4
            for p in range(4):
                pick[dest, p] = ref[inv_s[first + p]]
            return 0

        lax.fori_loop(0, Z, choose, 0)
        copies = []
        for d in range(1, Z):
            dest = lax.rem(z + d, Z)
            copies.append(
                send(
                    pick.at[dest], full.at[pl.ds(0, 4), z], z3s.at[kv, d], z3r.at[kv, d], at_z(d)
                )
            )
        for p in range(4):
            full[p, z] = pick[z, p]
        z3.append(copies)

    p_la.wait_recv()
    p_lb.wait_recv()
    grad_att(left, False)
    p_rb.wait_recv()
    p_ra.wait_recv()
    grad_att(right, False)
    fr.wait_recv()
    p_oa = forward(opp, lo, 0, 5)
    fl.wait_recv()
    p_ob = forward(opp, hi, 0, 6)
    p_oa.wait_recv()
    p_ob.wait_recv()
    grad_att(opp, False)
    ga_t[...] = ga_acc[...].astype(BF16).reshape(HEADS, HEAD, ROWS)

    for cp in loads[1:3] + loads[6:]:
        cp.wait()
    for copies in z3:
        for cp in copies:
            cp.wait_recv()
    kt_s[...] = kall[...].reshape(KEYS, HEAD).T
    vt_s[...] = vall[...].reshape(KEYS, HEAD).T

    def forward_head(h, _):
        keys = kall[...].reshape(KEYS, HEAD)
        st = dot(keys, q3[h], NT)
        s0 = st[:PROMPT]
        s1 = jnp.where(mask_s[...] != 0, st[PROMPT:], MASKED)
        top = jnp.maximum(jnp.max(s0, 0, keepdims=True), jnp.max(s1, 0, keepdims=True))
        e0 = jnp.exp2((s0 - top) * EXP_SCALE)
        e1 = jnp.exp2((s1 - top) * EXP_SCALE)
        total = jnp.sum(e0, 0, keepdims=True) + jnp.sum(e1, 0, keepdims=True)
        inverse = 1.0 / total
        pt_s[h, :PROMPT] = (e0 * inverse).astype(BF16)
        pt_s[h, PROMPT:] = (e1 * inverse).astype(BF16)
        probs = pt_s[h]
        grad = ga_t[h]
        out_t = dot(vt_s[...], probs)
        low = out_t.astype(BF16).astype(F32)
        delta_s[h] = jnp.sum(low * grad.astype(F32), 0, keepdims=True)
        att_s[:, pl.ds(pl.multiple_of(h * HEAD, HEAD), HEAD)] = out_t.T.astype(BF16)
        dv_acc[...] += dot(probs, grad, NT)
        return 0

    lax.fori_loop(0, HEADS, forward_head, 0)

    def reduce_start(kv, grad, g_ref, rg):
        g_ref[...] = grad[:PROMPT].astype(BF16).reshape(4, Z, 16, HEAD)
        rg[z] = g_ref[:, z]
        return [
            send(
                g_ref.at[:, lax.rem(z + d, Z)], rg.at[z], b3s.at[kv, d], b3r.at[kv, d], at_z(d)
            )
            for d in range(1, Z)
        ]

    b3 = [None, None]
    b2 = [None, None]
    b1 = [None, None]
    b3[1] = reduce_start(1, dv_acc[...], g_v, rg_v)
    gkv_s[1] = dv_acc[PROMPT:].astype(BF16)
    stores = [pltpu.make_async_copy(gkv_s.at[1], gv_h, loc.at[14])]
    stores[-1].start()

    def backward_head(h, _):
        values = vall[...].reshape(KEYS, HEAD)
        grad_p = dot(values, ga_t[h])
        low = (pt_s[h].astype(F32) * (grad_p - delta_s[h])).astype(BF16)
        ds_s[h] = low
        dk_acc[...] += dot(low, q3[h])
        return 0

    lax.fori_loop(0, HEADS, backward_head, 0)
    grad_k = dk_acc[...] * SCALE
    b3[0] = reduce_start(0, grad_k, g_k, rg_k)
    gkv_s[0] = grad_k[PROMPT:].astype(BF16)
    stores.append(pltpu.make_async_copy(gkv_s.at[0], gk_h, loc.at[15]))
    stores[-1].start()

    def query_head(h, _):
        dq = dot(kt_s[...], ds_s[h])
        gq_s[:, pl.ds(pl.multiple_of(h * HEAD, HEAD), HEAD)] = (dq.T * SCALE).astype(BF16)
        return 0

    lax.fori_loop(0, HEADS, query_head, 0)
    stores.append(pltpu.make_async_copy(gq_s, gq_h, loc.at[16]))
    stores[-1].start()

    def reduce_z(kv, rg, qs, rq):
        for cp in b3[kv]:
            cp.wait_recv()

        def slot(j, _):
            s = own_s[j]
            group, piece = s // 4, s % 4
            total = jnp.zeros((16, HEAD), F32)
            for source in range(Z):
                hit = jnp.full((16, HEAD), grp_s[y * Z + source], jnp.int32) == group
                total += jnp.where(hit, rg[source, piece].astype(F32), 0.0)
            qs[j] = total.astype(BF16)
            return 0

        lax.fori_loop(0, Y * Z, slot, 0)
        rq[y] = qs[pl.ds(y * Z, Z)]
        b2[kv] = [
            send(
                qs.at[pl.ds(lax.rem(y + d, Y) * Z, Z)],
                rq.at[y],
                b2s.at[kv, d],
                b2r.at[kv, d],
                at_y(d),
            )
            for d in range(1, Y)
        ]

    def reduce_y(kv, rq, u, fin):
        for cp in b2[kv]:
            cp.wait_recv()
        total = rq[0].astype(F32)
        for source in range(1, Y):
            total += rq[source].astype(F32)
        u[...] = total.astype(BF16)
        fin[z] = u[z]
        b1[kv] = [
            send(u.at[lax.rem(z + d, Z)], fin.at[z], b1s.at[kv, d], b1r.at[kv, d], at_z(d))
            for d in range(1, Z)
        ]

    def reduce_end(kv, fin, out, dst):
        for cp in b1[kv]:
            cp.wait_recv()
        out[...] = fin[...].astype(F32)
        stores.append(pltpu.make_async_copy(out, dst, loc.at[17 + kv]))
        stores[-1].start()

    core = [None] * CH
    one = [None] * CH
    two = [None] * CH

    def product(n):
        def step(i, _):
            cols = pl.ds(pl.multiple_of(n * CW + i * SUB, SUB), SUB)
            part = dot(att_s[...], w_s[:, cols]).astype(BF16)
            pb[n, :, :, :, pl.ds(pl.multiple_of(i * SUB, SUB), SUB)] = part.reshape(X, 2, 32, SUB)
            return 0

        lax.fori_loop(0, CW // SUB, step, 0)
        core[n] = send(pb.at[n, :, 1 - c], rb1.at[n], cs.at[n], cr.at[n], partner)

    def ring_one(n):
        core[n].wait_recv()
        for d in range(X):
            b = lax.rem(x + d, X)
            acc[n, d] = (pb[n, b, c].astype(F32) + rb1[n, b].astype(F32)).astype(BF16)
        one[n] = (
            send(acc.at[n, 2, pl.ds(0, 16)], rs1.at[n, 0], r1s.at[n, 0], r1r.at[n, 0], to_right),
            send(acc.at[n, 2, pl.ds(16, 16)], rs1.at[n, 1], r1s.at[n, 1], r1r.at[n, 1], to_left),
        )

    def ring_two(n):
        one[n][0].wait_recv()
        acc[n, 1, :16] = (acc[n, 1, :16].astype(F32) + rs1[n, 0].astype(F32)).astype(BF16)
        first = send(acc.at[n, 1], rs2.at[n, 0], r2s.at[n, 0], r2r.at[n, 0], to_right)
        one[n][1].wait_recv()
        acc[n, 3, 16:] = (acc[n, 3, 16:].astype(F32) + rs1[n, 1].astype(F32)).astype(BF16)
        two[n] = (
            first,
            send(acc.at[n, 3], rs2.at[n, 1], r2s.at[n, 1], r2r.at[n, 1], to_left),
        )

    def ring_end(n):
        two[n][0].wait_recv()
        two[n][1].wait_recv()
        total = acc[n, 0].astype(F32) + rs2[n, 0].astype(F32) + rs2[n, 1].astype(F32)
        bo_s[:, n * CW : (n + 1) * CW] = total.astype(BF16)

    product(0)
    product(1)
    ring_one(0)
    reduce_z(1, rg_v, qs_v, rq_v)
    product(2)
    ring_one(1)
    product(3)
    ring_one(2)
    reduce_z(0, rg_k, qs_k, rq_k)
    ring_two(0)
    ring_one(3)
    ring_two(1)
    reduce_y(1, rq_v, u_v, fin_v)
    ring_two(2)
    ring_two(3)
    reduce_y(0, rq_k, u_k, fin_k)
    ring_end(0)
    ring_end(1)
    reduce_end(1, fin_v, out_v, gpv_h)
    ring_end(2)
    ring_end(3)
    stores.append(pltpu.make_async_copy(bo_s, bo_h, loc.at[19]))
    stores[-1].start()
    reduce_end(0, fin_k, out_k, gpk_h)
    for cp in sent:
        cp.wait_send()
    for cp in stores:
        cp.wait()


def local(
    queries, keys, values, prompt_keys, prompt_values,
    lengths, owner_slice, device_group, out_weight, cotangent,
):
    smem = pl.BlockSpec(memory_space=pltpu.SMEM)
    hbm = pl.BlockSpec(memory_space=pl.ANY)
    vm = pltpu.VMEM
    dma = pltpu.SemaphoreType.DMA
    tile = (16, HEAD)
    scratch = [
        vm((HEADS * HEAD, D), BF16),
        vm((X, ROWS, PAIR), BF16),
        vm((HEADS * HEAD, ROWS), F32),
        vm((HEADS, HEAD, ROWS), BF16),
        vm((HEADS, ROWS, HEAD), BF16),
        vm((6, Z) + tile, BF16),
        vm((6, Z) + tile, BF16),
        vm((HEAD, KEYS), BF16),
        vm((HEAD, KEYS), BF16),
        vm((Y * Z,) + tile, BF16),
        vm((Y * Z,) + tile, BF16),
        vm((Z, 4) + tile, BF16),
        vm((Z, 4) + tile, BF16),
        vm((ROWS, ROWS), jnp.int32),
        vm((HEADS, KEYS, ROWS), BF16),
        vm((HEADS, KEYS, ROWS), BF16),
        vm((HEADS, 1, ROWS), F32),
        vm((ROWS, HEADS * HEAD), BF16),
        vm((KEYS, HEAD), F32),
        vm((KEYS, HEAD), F32),
        vm((ROWS, HEADS * HEAD), BF16),
        vm((2, ROWS, HEAD), BF16),
        vm((4, Z) + tile, BF16),
        vm((4, Z) + tile, BF16),
        vm((Z, 4) + tile, BF16),
        vm((Z, 4) + tile, BF16),
        vm((Y * Z,) + tile, BF16),
        vm((Y * Z,) + tile, BF16),
        vm((Y, Z) + tile, BF16),
        vm((Y, Z) + tile, BF16),
        vm((Z,) + tile, BF16),
        vm((Z,) + tile, BF16),
        vm((Z,) + tile, BF16),
        vm((Z,) + tile, BF16),
        vm((Z,) + tile, F32),
        vm((Z,) + tile, F32),
        vm((CH, X, 2, 32, CW), BF16),
        vm((CH, X, 32, CW), BF16),
        vm((CH, X, 32, CW), BF16),
        vm((CH, 2, 16, CW), BF16),
        vm((CH, 2, 32, CW), BF16),
        vm((32, D), BF16),
        pltpu.SMEM((Y * Z,), jnp.int32),
        dma((20,)),
        dma((2, Z)), dma((2, Z)),
        dma((2, Y)), dma((2, Y)),
        dma((2, Z)), dma((2, Z)),
        dma((6,)), dma((6,)),
        dma((7,)), dma((7,)),
        dma((2, Z)), dma((2, Z)),
        dma((2, Y)), dma((2, Y)),
        dma((2, Z)), dma((2, Z)),
        dma((CH,)), dma((CH,)),
        dma((CH, 2)), dma((CH, 2)),
        dma((CH, 2)), dma((CH, 2)),
    ]
    shape = jax.ShapeDtypeStruct
    outs = pl.pallas_call(
        kernel,
        out_shape=(
            shape((32, D), BF16),
            shape((ROWS, HEADS * HEAD), BF16),
            shape((ROWS, HEAD), BF16),
            shape((ROWS, HEAD), BF16),
            shape((Z,) + tile, F32),
            shape((Z,) + tile, F32),
        ),
        in_specs=[smem] * 3 + [hbm] * 7,
        out_specs=[hbm] * 6,
        scratch_shapes=scratch,
        compiler_params=pltpu.CompilerParams(
            collective_id=0, has_side_effects=True, vmem_limit_bytes=58 * 1024 * 1024
        ),
        name="attention_block",
    )(
        lengths,
        owner_slice,
        device_group,
        queries,
        keys.reshape(2, Z, 16, HEAD),
        values.reshape(2, Z, 16, HEAD),
        prompt_keys.reshape(Z, 16, HEAD),
        prompt_values.reshape(Z, 16, HEAD),
        out_weight,
        cotangent,
    )
    return outs[:4] + (outs[4].reshape(128, HEAD), outs[5].reshape(128, HEAD))


def solution(mesh):
    placed = (
        P("dp", "tensor"),
        P("dp", "tensor"),
        P("dp", "tensor"),
        P("dp", "tensor"),
        P("dp", "tensor"),
        P("dp", None),
        P(),
        P(),
        P("tensor", None),
        P("dp", "tensor"),
    )
    return jax.shard_map(
        local,
        mesh=mesh,
        in_specs=placed,
        out_specs=(
            P(("dp", "tensor"), None),
            P("dp", "tensor"),
            P("dp", "tensor"),
            P("dp", "tensor"),
            P("dp", "tensor"),
            P("dp", "tensor"),
        ),
        check_vma=False,
    )
```

time: 506 us -> 74.6 us (0.15)
  waiting for transfers between devices: 382 us -> 0 us
  Pallas kernels: 0 us -> 64.1 us
  matrix products: 36.8 us -> 0 us
  other arithmetic: 33.4 us -> 0 us
  local copies, waits for them, and re-layouts: 36.4 us -> 9.47 us
  between operations: 14.1 us -> 0.65 us
    reduce_scatter x2 -> x0, waiting for transfers between devices: 240 us -> none  [the longest x1 196 us: local(): lax.psum_scatter(jnp.where(match[:, None], jnp.take(partial_value, source...]
    all_gather x3 -> x0, waiting for transfers between devices: 140 us -> none  [the longest x1 64.5 us: local(): lax.all_gather(prompt_values, 'dp', axis=0, tiled=True)]
    pallas_call x0 -> x1, Pallas kernels: none -> 64.1 us  [local(): pl.pallas_call(kernel, out_shape=(shape((32, D), BF16), shape((ROWS, HEAD...]
    dot_general x10 -> x0, matrix products: 36.8 us -> none  [the longest x1 9.54 us: local(): jnp.dot(attended, out_weight, preferred_element_type=jnp.float32)]
    gather x3 -> x0, local copies, waits for them, and re-layouts: 18.5 us -> none  [the longest x1 14.6 us: local(): jnp.take(partial_value, source, axis=0)]
    and x2 -> x0, other arithmetic: 16.6 us -> none  [the longest x1 16.5 us: local(): jnp.take(partial_value, source, axis=0)]
    gather x27 -> x0, other arithmetic: 6.41 us -> none  [the longest x26 5.8 us: local(): held = owner_slice[spot // slice_rows]]
    convert_element_type x2 -> x0, other arithmetic: 6.02 us -> none  [the longest x1 4.17 us: local(): jnp.where(match[:, None], jnp.take(partial_value, source, axis=0), jnp.fl...]
  transfers between devices with their start and end apart: 5 -> 0, of which waited for: 5 -> 0; matrix products, arithmetic and copies ran while one was open for 12% -> 0% of each run, Pallas kernels for 0% -> 0%
where the time goes in v1:
time: 74.6 us; the launch traced here: 74.2 us
  Pallas kernels  64.1 us (86%)
  local copies, waits for them, and re-layouts  9.47 us (13%)
    pallas_call x1, Pallas kernels, local(): pl.pallas_call(kernel, out_shape=(shape((32, D), BF16), shape((ROWS, HEAD...  64.1 us
    unnamed x6, local copies, waits for them, and re-layouts  9.47 us

profile of v1, /device:TPU:1, one launch (start us, length us, event | category | flops | bytes accessed | tf_op | source)
XLA Modules:
  0.0 74.2 jit_solution(8851161622480082472)
XLA Ops:
  0.6 64.1 %attention_block.1 = (bf16[32,5120]{1,0:T(8,128)(2,1)}, bf16[256,1024]{1,0:T(8,128)(2,1)}, bf16[256,128]{1,0:T(8,128)(2,1)}, bf16[256,128]{1,0:T(8,128)(2,1)}, f...) custom-call(s32[1,4]{1,0:T(1,128)} %len_s.1, s32[32]{0:T(128)} %own_s.1, s32[32]{0:T(128)} %grp_s.1, bf16[256,1024]{1,0:T(8,128)(2,1)} %q_h.1, ...), custom_call_target="tpu_custom_call" | custom-call | tf_op jit(solution)/shard_map/attention_block/pallas_call | solution.py:478
  64.7 1.7 %copy.22 = bf16[32,5120]{1,0:T(8,128)(2,1)} copy(bf16[32,5120]{1,0:T(8,128)(2,1)} %get-tuple-element.24) | data formatting | bytes 655360
  66.5 1.9 %copy.23 = bf16[256,1024]{1,0:T(8,128)(2,1)} copy(bf16[256,1024]{1,0:T(8,128)(2,1)} %get-tuple-element.25) | data formatting | bytes 1048576
  68.3 1.5 %copy.24 = bf16[256,128]{1,0:T(8,128)(2,1)} copy(bf16[256,128]{1,0:T(8,128)(2,1)} %get-tuple-element.26) | data formatting | bytes 131072
  69.8 1.5 %copy.25 = bf16[256,128]{1,0:T(8,128)(2,1)} copy(bf16[256,128]{1,0:T(8,128)(2,1)} %get-tuple-element.27) | data formatting | bytes 131072
  71.3 1.5 %copy.26 = f32[128,128]{1,0:T(8,128)} copy(f32[128,128]{1,0:T(8,128)} %bitcast.9) | data formatting | bytes 131072
  72.8 1.5 %copy.27 = f32[128,128]{1,0:T(8,128)} copy(f32[128,128]{1,0:T(8,128)} %bitcast.8) | data formatting | bytes 131072
